TPU v7x, 32 devices: a whole 2x2x4 slice. The times are simulated.
32 devices in a mesh: sta: 8 (over z, x), slab: 4 (over y, core).
Axes of the slice: x: 2, y: 2, z: 4, core: 2. Of those that a mesh axis runs over, the one named last changes fastest.
Arguments:
- green_fields: bfloat16 [2, 16, 64, 4096], P(None, 'sta', 'slab'), may hold values from -6 to 6
- pair_list: int32 [64, 2], replicated, may hold values from 0 to 15
- pair_values: float32 [2, 64], replicated, may hold values from -6 to 6
- noise_map: float32 [64, 4096], P('slab'), may hold values from 0.1 to 1
- wave_square: float32 [64, 4096], P('slab'), may hold values from 0.1 to 1.5
- station_cell: int32 [16], P('sta'), may hold values from 0 to 262143
Outputs:
- adjoint_field: float32 [2, 16, 64, 4096], P(None, 'sta', 'slab')
Inputs may be any that keep to these rules, and one draw needn't show every extreme that they name: `pair_list`: pairs may repeat and may name one station twice; repeated entries add up. `station_cell`: index = depth layer * 64 * 64 + lateral index; stations may share a cell.
All inputs are finite; a program needn't handle non-finite values.
Results may differ from a plain program's by a relative error of at most 0.004.
Values may be sent and summed in bfloat16 or wider, within the bound.
A program may use at most 64 MiB of HBM per device.

v0:
```python
import jax
import jax.numpy as jnp
from jax import lax
from jax.sharding import PartitionSpec as P

GY = 64
SWEEPS = 6


damping = 0.3
relaxation = 0.8
point_size = 2.0


def extended(block, sides, width):
    for axis, dim in sides:
        count = lax.axis_size(axis)
        forward = [(i, i + 1) for i in range(count - 1)]
        backward = [(target, source) for source, target in forward]
        low = lax.ppermute(
            lax.slice_in_dim(block, block.shape[dim] - width, None, axis=dim), axis, forward
        )
        high = lax.ppermute(lax.slice_in_dim(block, 0, width, axis=dim), axis, backward)
        block = jnp.concatenate([low, block, high], axis=dim)
    return block


def build_resid(pair_list, pair_values, count):
    labels = jnp.arange(count, dtype=jnp.int32)
    first = (pair_list[:, 0:1] == labels[None, :]).astype(jnp.float32)
    second = (pair_list[:, 1:2] == labels[None, :]).astype(jnp.float32)
    real_w = pair_values[0][:, None]
    imag_w = pair_values[1][:, None]
    highest = lax.Precision.HIGHEST
    resid_real = jnp.dot(
        first.T, real_w * second, precision=highest, preferred_element_type=jnp.float32
    ) + jnp.dot(second.T, real_w * first, precision=highest, preferred_element_type=jnp.float32)
    resid_imag = jnp.dot(
        first.T, imag_w * second, precision=highest, preferred_element_type=jnp.float32
    ) - jnp.dot(second.T, imag_w * first, precision=highest, preferred_element_type=jnp.float32)
    resid_real = resid_real.astype(jnp.bfloat16)
    resid_imag = resid_imag.astype(jnp.bfloat16)
    upper = jnp.concatenate([resid_real, -resid_imag], axis=1)
    lower = jnp.concatenate([resid_imag, resid_real], axis=1)
    return jnp.concatenate([upper, lower], axis=0)


def lateral(field, width_y):
    width = field.shape[-1]
    zeros_pad = [(0, 0)] * (field.ndim - 1)
    padded = jnp.pad(field, zeros_pad + [(width_y, width_y)])
    along_x = padded[..., :width] + padded[..., 2 * width_y :]
    column = jnp.arange(width, dtype=jnp.int32) % width_y
    stepped = jnp.pad(field, zeros_pad + [(1, 1)])
    left = stepped[..., :width] * (column != 0).astype(jnp.float32)
    right = stepped[..., 2:] * (column != width_y - 1).astype(jnp.float32)
    return along_x + left + right


def scales_from(wave):
    diag_real = 6.0 - wave
    denom = diag_real * diag_real + damping * wave * (damping * wave)
    return (relaxation * diag_real / denom, relaxation * damping * wave / denom)


def relax(padded, source, wave, scale_real, scale_imag, width_y):
    inner = padded[:, :, 1:-1]
    near = lateral(inner, width_y) + padded[:, :, :-2] + padded[:, :, 2:]
    real_in = inner[0]
    imag_in = inner[1]
    applied_real = 6.0 * real_in - near[0] - wave * (real_in - damping * imag_in)
    applied_imag = 6.0 * imag_in - near[1] - wave * (damping * real_in + imag_in)
    rest_real = source[0] - applied_real
    rest_imag = source[1] - applied_imag
    return jnp.stack(
        [
            real_in + scale_real * rest_real - scale_imag * rest_imag,
            imag_in + scale_real * rest_imag + scale_imag * rest_real,
        ]
    )


def local(green_fields, pair_list, pair_values, noise_map, wave_square, station_cell):
    owned = green_fields.shape[1]
    depth = green_fields.shape[2]
    cells = green_fields.shape[3]
    count = owned * lax.axis_size("sta")
    big = build_resid(pair_list, pair_values, count)
    pieces = lax.all_to_all(green_fields, "sta", split_axis=3, concat_axis=1, tiled=True)
    layout = pieces.shape
    flat = pieces.reshape(2 * layout[1], layout[2] * layout[3])
    mixed = jnp.dot(big, flat, preferred_element_type=jnp.float32).astype(jnp.bfloat16)
    moved = mixed.reshape(layout)
    adjoint = lax.all_to_all(moved, "sta", split_axis=1, concat_axis=3, tiled=True)
    offset = lax.axis_index("slab") * (depth * cells)
    flat_cells = jnp.arange(depth * cells, dtype=jnp.int32) + offset
    spot = (flat_cells[None, :] == station_cell[:, None]).astype(jnp.float32).reshape(
        owned, depth, cells
    ) * point_size
    source = noise_map[None, None] * adjoint.astype(jnp.float32)
    source = jnp.stack([source[0] + spot, source[1]])
    field = jnp.zeros((2, owned, depth, cells), jnp.float32)
    scale_real, scale_imag = scales_from(wave_square)
    for repeat in range(SWEEPS):
        padded = extended(field, (("slab", 2),), 1)
        field = relax(padded, source, wave_square, scale_real, scale_imag, GY)
    return field


def solution(mesh):
    placed = (P(None, "sta", "slab", None), P(), P(), P("slab", None), P("slab", None), P("sta"))
    return jax.shard_map(
        local, mesh=mesh, in_specs=placed, out_specs=P(None, "sta", "slab", None), check_vma=False
    )
```

profile of v0, /device:TPU:1, one launch (start us, length us, event | category | flops | bytes accessed | tf_op | source)
XLA Modules:
  0.0 125.9 jit_solution(9483323790944660436)
XLA Ops:
  0.0 4.5 %collective-permute-start = (f32[2,2,1,4096]{3,2,1,0:T(1,128)S(1)}, f32[2,2,1,4096]{3,2,1,0:T(1,128)S(1)}, u32[]{:S(2)}, u32[]{:S(2)}) collective-permute-start(f32[2,2,1,4096]{3,2,1,0:T(1,128)S(1)} %broadcast.574), channel_id=1, source_target_pairs={{0,1},{1,2},{2,3},{4,5},{5,6},{6,7},{8,9},{9,10},{10,11},{12,13},{... | collective-permute-start | bytes 196616 | tf_op jit(solution)/shard_map/ppermute | solution.py:20
  4.6 1.9 %collective-permute-start.1 = (f32[2,2,1,4096]{3,2,1,0:T(1,128)S(1)}, f32[2,2,1,4096]{3,2,1,0:T(1,128)S(1)}, u32[]{:S(2)}, u32[]{:S(2)}) collective-permute-start(f32[2,2,1,4096]{3,2,1,0:T(1,128)S(1)} %broadcast.574), channel_id=1, source_target_pairs={{1,0},{2,1},{3,2},{5,4},{6,5},{7,6},{9,8},{10,9},{11,10},{13,12},{... | collective-permute-start | bytes 196616 | tf_op jit(solution)/shard_map/ppermute | solution.py:23
  6.5 9.1 %copy.10 = bf16[2,2,16,4096]{2,1,0,3:T(2,128)(2,1)} copy(bf16[2,2,16,4096]{3,2,1,0:T(8,128)(2,1)} %param.6) | data formatting | bytes 1048576 | tf_op args[0]
  15.6 6.5 %reshape.92 = bf16[8,2,16384]{2,1,0:T(2,128)(2,1)} reshape(bf16[4096,2,2,16]{3,2,1,0:T(2,128)(2,1)} %bitcast.26) | data formatting | bytes 1048576
  22.1 5.7 %all-to-all-start = ((bf16[8,2,16384]{2,1,0:T(2,128)(2,1)}), bf16[8,2,16384]{2,1,0:T(2,128)(2,1)S(1)}, u32[]{:S(2)}, u32[]{:S(2)}) async-start(bf16[8,2,16384]{2,1,0:T(2,128)(2,1)} %reshape.92), calls=%async_computation | async-start | bytes 1048576 | tf_op jit(solution)/shard_map/all_to_all | solution.py:89
  29.1 12.3 %all-to-all-done = bf16[8,2,16384]{2,1,0:T(2,128)(2,1)S(1)} async-done(((bf16[8,2,16384]{2,1,0:T(2,128)(2,1)}), bf16[8,2,16384]{2,1,0:T(2,128)(2,1)S(1)}, u32[]{:S(2)}, u32[]{:S(2)}) %all-to-all-start) | async-done | bytes 524320 | tf_op jit(solution)/shard_map/all_to_all | solution.py:89
  41.3 4.1 %reshape.93 = bf16[4096,2,2,16]{3,2,1,0:T(2,128)(2,1)} reshape(bf16[8,2,16384]{2,1,0:T(2,128)(2,1)S(1)} %all-to-all-done) | data formatting | bytes 1048576
  45.4 8.9 %copy.11 = bf16[2,2,16,8,512]{4,2,1,3,0:T(8,128)(2,1)S(1)} copy(bf16[2,2,16,8,512]{2,1,0,4,3:T(2,128)(2,1)} %bitcast.25) | data formatting | bytes 1048576 | tf_op jit(solution)/shard_map/all_to_all | solution.py:89
  56.0 3.6 %all-to-all-start.1 = ((bf16[2,16,16,512]{3,2,0,1:T(8,128)(2,1)}), bf16[2,16,16,512]{3,2,0,1:T(8,128)(2,1)S(1)}, u32[]{:S(2)}, u32[]{:S(2)}) async-start(bf16[2,16,16,512]{3,2,0,1:T(8,128)(2,1)} %copy.12), calls=%async_computation.1 | async-start | bytes 1048576 | tf_op jit(solution)/shard_map/all_to_all | solution.py:94
  60.8 12.3 %all-to-all-done.1 = bf16[2,16,16,512]{3,2,0,1:T(8,128)(2,1)S(1)} async-done(((bf16[2,16,16,512]{3,2,0,1:T(8,128)(2,1)}), bf16[2,16,16,512]{3,2,0,1:T(8,128)(2,1)S(1)}, u32[]{:S(2)}, u32[]{:S(2)}) %all-to-all-start.1) | async-done | bytes 524320 | tf_op jit(solution)/shard_map/all_to_all | solution.py:94
  76.9 4.1 %collective-permute-start.2 = (f32[2,2,1,4096]{3,2,1,0:T(1,128)S(1)}, f32[2,2,1,4096]{3,2,1,0:T(1,128)S(1)}, u32[]{:S(2)}, u32[]{:S(2)}) collective-permute-start(f32[2,2,1,4096]{3,2,1,0:T(1,128)S(1)} %get-tuple-element.25), channel_id=1, source_target_pairs={{0,1},{1,2},{2,3},{4,5},{5,6},{6,7},{8,9},{9,10},{10,11},{12,13},{... | collective-permute-start | bytes 196616 | tf_op jit(solution)/shard_map/ppermute | solution.py:20
  81.0 1.9 %collective-permute-start.3 = (f32[2,2,1,4096]{3,2,1,0:T(1,128)S(1)}, f32[2,2,1,4096]{3,2,1,0:T(1,128)S(1)}, u32[]{:S(2)}, u32[]{:S(2)}) collective-permute-start(f32[2,2,1,4096]{3,2,1,0:T(1,128)S(1)} %get-tuple-element.26), channel_id=1, source_target_pairs={{1,0},{2,1},{3,2},{5,4},{6,5},{7,6},{9,8},{10,9},{11,10},{13,12},{... | collective-permute-start | bytes 196616 | tf_op jit(solution)/shard_map/ppermute | solution.py:23
  83.1 3.6 %collective-permute-done.3 = f32[2,2,1,4096]{3,2,1,0:T(1,128)S(1)} collective-permute-done((f32[2,2,1,4096]{3,2,1,0:T(1,128)S(1)}, f32[2,2,1,4096]{3,2,1,0:T(1,128)S(1)}, u32[]{:S(2)}, u32[]{:S(2)}) %collective-permute-start.3) | collective-permute-done | bytes 65568 | tf_op jit(solution)/shard_map/ppermute | solution.py:23
  88.3 1.9 %collective-permute-start.4 = (f32[2,2,1,4096]{3,2,1,0:T(1,128)S(1)}, f32[2,2,1,4096]{3,2,1,0:T(1,128)S(1)}, u32[]{:S(2)}, u32[]{:S(2)}) collective-permute-start(f32[2,2,1,4096]{3,2,1,0:T(1,128)S(1)} %get-tuple-element.23), channel_id=1, source_target_pairs={{0,1},{1,2},{2,3},{4,5},{5,6},{6,7},{8,9},{9,10},{10,11},{12,13},{... | collective-permute-start | bytes 196616 | tf_op jit(solution)/shard_map/ppermute | solution.py:20
  90.2 2.4 %collective-permute-start.5 = (f32[2,2,1,4096]{3,2,1,0:T(1,128)S(1)}, f32[2,2,1,4096]{3,2,1,0:T(1,128)S(1)}, u32[]{:S(2)}, u32[]{:S(2)}) collective-permute-start(f32[2,2,1,4096]{3,2,1,0:T(1,128)S(1)} %get-tuple-element.24), channel_id=1, source_target_pairs={{1,0},{2,1},{3,2},{5,4},{6,5},{7,6},{9,8},{10,9},{11,10},{13,12},{... | collective-permute-start | bytes 196616 | tf_op jit(solution)/shard_map/ppermute | solution.py:23
  92.7 3.1 %collective-permute-done.5 = f32[2,2,1,4096]{3,2,1,0:T(1,128)S(1)} collective-permute-done((f32[2,2,1,4096]{3,2,1,0:T(1,128)S(1)}, f32[2,2,1,4096]{3,2,1,0:T(1,128)S(1)}, u32[]{:S(2)}, u32[]{:S(2)}) %collective-permute-start.5) | collective-permute-done | bytes 65568 | tf_op jit(solution)/shard_map/ppermute | solution.py:23
  97.4 1.9 %collective-permute-start.6 = (f32[2,2,1,4096]{3,2,1,0:T(1,128)S(1)}, f32[2,2,1,4096]{3,2,1,0:T(1,128)S(1)}, u32[]{:S(2)}, u32[]{:S(2)}) collective-permute-start(f32[2,2,1,4096]{3,2,1,0:T(1,128)S(1)} %get-tuple-element.21), channel_id=1, source_target_pairs={{0,1},{1,2},{2,3},{4,5},{5,6},{6,7},{8,9},{9,10},{10,11},{12,13},{... | collective-permute-start | bytes 196616 | tf_op jit(solution)/shard_map/ppermute | solution.py:20
  99.4 2.6 %collective-permute-start.7 = (f32[2,2,1,4096]{3,2,1,0:T(1,128)S(1)}, f32[2,2,1,4096]{3,2,1,0:T(1,128)S(1)}, u32[]{:S(2)}, u32[]{:S(2)}) collective-permute-start(f32[2,2,1,4096]{3,2,1,0:T(1,128)S(1)} %get-tuple-element.22), channel_id=1, source_target_pairs={{1,0},{2,1},{3,2},{5,4},{6,5},{7,6},{9,8},{10,9},{11,10},{13,12},{... | collective-permute-start | bytes 196616 | tf_op jit(solution)/shard_map/ppermute | solution.py:23
  102.0 2.9 %collective-permute-done.7 = f32[2,2,1,4096]{3,2,1,0:T(1,128)S(1)} collective-permute-done((f32[2,2,1,4096]{3,2,1,0:T(1,128)S(1)}, f32[2,2,1,4096]{3,2,1,0:T(1,128)S(1)}, u32[]{:S(2)}, u32[]{:S(2)}) %collective-permute-start.7) | collective-permute-done | bytes 65568 | tf_op jit(solution)/shard_map/ppermute | solution.py:23
  106.6 1.9 %collective-permute-start.8 = (f32[2,2,1,4096]{3,2,1,0:T(1,128)S(1)}, f32[2,2,1,4096]{3,2,1,0:T(1,128)S(1)}, u32[]{:S(2)}, u32[]{:S(2)}) collective-permute-start(f32[2,2,1,4096]{3,2,1,0:T(1,128)S(1)} %get-tuple-element.19), channel_id=1, source_target_pairs={{0,1},{1,2},{2,3},{4,5},{5,6},{6,7},{8,9},{9,10},{10,11},{12,13},{... | collective-permute-start | bytes 196616 | tf_op jit(solution)/shard_map/ppermute | solution.py:20
  108.5 2.4 %collective-permute-start.9 = (f32[2,2,1,4096]{3,2,1,0:T(1,128)S(1)}, f32[2,2,1,4096]{3,2,1,0:T(1,128)S(1)}, u32[]{:S(2)}, u32[]{:S(2)}) collective-permute-start(f32[2,2,1,4096]{3,2,1,0:T(1,128)S(1)} %get-tuple-element.20), channel_id=1, source_target_pairs={{1,0},{2,1},{3,2},{5,4},{6,5},{7,6},{9,8},{10,9},{11,10},{13,12},{... | collective-permute-start | bytes 196616 | tf_op jit(solution)/shard_map/ppermute | solution.py:23
  111.0 3.1 %collective-permute-done.9 = f32[2,2,1,4096]{3,2,1,0:T(1,128)S(1)} collective-permute-done((f32[2,2,1,4096]{3,2,1,0:T(1,128)S(1)}, f32[2,2,1,4096]{3,2,1,0:T(1,128)S(1)}, u32[]{:S(2)}, u32[]{:S(2)}) %collective-permute-start.9) | collective-permute-done | bytes 65568 | tf_op jit(solution)/shard_map/ppermute | solution.py:23
  117.7 2.4 %collective-permute-start.11 = (f32[2,2,1,4096]{3,2,1,0:T(1,128)S(1)}, f32[2,2,1,4096]{3,2,1,0:T(1,128)S(1)}, u32[]{:S(2)}, u32[]{:S(2)}) collective-permute-start(f32[2,2,1,4096]{3,2,1,0:T(1,128)S(1)} %get-tuple-element.18), channel_id=1, source_target_pairs={{1,0},{2,1},{3,2},{5,4},{6,5},{7,6},{9,8},{10,9},{11,10},{13,12},{... | collective-permute-start | bytes 196616 | tf_op jit(solution)/shard_map/ppermute | solution.py:23
  120.2 3.1 %collective-permute-done.11 = f32[2,2,1,4096]{3,2,1,0:T(1,128)S(1)} collective-permute-done((f32[2,2,1,4096]{3,2,1,0:T(1,128)S(1)}, f32[2,2,1,4096]{3,2,1,0:T(1,128)S(1)}, u32[]{:S(2)}, u32[]{:S(2)}) %collective-permute-start.11) | collective-permute-done | bytes 65568 | tf_op jit(solution)/shard_map/ppermute | solution.py:23
  (59 shorter events, 19.2 us)
Async XLA Ops:
  0.0 59.5 %collective-permute-start = (f32[2,2,1,4096]{3,2,1,0:T(1,128)S(1)}, f32[2,2,1,4096]{3,2,1,0:T(1,128)S(1)}, u32[]{:S(2)}, u32[]{:S(2)}) collective-permute-start(f32[2,2,1,4096]{3,2,1,0:T(1,128)S(1)} %broadcast.574), channel_id=1, source_target_pairs={{0,1},{1,2},{2,3},{4,5},{5,6},{6,7},{8,9},{9,10},{10,11},{12,13},{... | collective-permute-start | bytes 196616 | tf_op jit(solution)/shard_map/ppermute | solution.py:20
  4.6 54.9 %collective-permute-start.1 = (f32[2,2,1,4096]{3,2,1,0:T(1,128)S(1)}, f32[2,2,1,4096]{3,2,1,0:T(1,128)S(1)}, u32[]{:S(2)}, u32[]{:S(2)}) collective-permute-start(f32[2,2,1,4096]{3,2,1,0:T(1,128)S(1)} %broadcast.574), channel_id=1, source_target_pairs={{1,0},{2,1},{3,2},{5,4},{6,5},{7,6},{9,8},{10,9},{11,10},{13,12},{... | collective-permute-start | bytes 196616 | tf_op jit(solution)/shard_map/ppermute | solution.py:23
  22.1 5.7 %copy-start.1 = (s32[64,2]{0,1:T(2,128)S(1)}, s32[64,2]{0,1:T(2,128)}, u32[]{:S(2)}) copy-start(s32[64,2]{0,1:T(2,128)} %param.7) | copy-start | bytes 1540
  22.1 5.7 %copy-start.2 = (f32[2,64]{1,0:T(2,128)S(1)}, f32[2,64]{1,0:T(2,128)}, u32[]{:S(2)}) copy-start(f32[2,64]{1,0:T(2,128)} %param.8) | copy-start | bytes 1540
  22.1 6.9 %copy-start = (f32[16,4096]{1,0:T(8,128)S(1)}, f32[16,4096]{1,0:T(8,128)}, u32[]{:S(2)}) copy-start(f32[16,4096]{1,0:T(8,128)} %param.10) | copy-start | bytes 786436
  22.1 19.2 %all-to-all-start = ((bf16[8,2,16384]{2,1,0:T(2,128)(2,1)}), bf16[8,2,16384]{2,1,0:T(2,128)(2,1)S(1)}, u32[]{:S(2)}, u32[]{:S(2)}) async-start(bf16[8,2,16384]{2,1,0:T(2,128)(2,1)} %reshape.92), calls=%async_computation | async-start | bytes 1048576 | tf_op jit(solution)/shard_map/all_to_all | solution.py:89
  56.0 17.1 %all-to-all-start.1 = ((bf16[2,16,16,512]{3,2,0,1:T(8,128)(2,1)}), bf16[2,16,16,512]{3,2,0,1:T(8,128)(2,1)S(1)}, u32[]{:S(2)}, u32[]{:S(2)}) async-start(bf16[2,16,16,512]{3,2,0,1:T(8,128)(2,1)} %copy.12), calls=%async_computation.1 | async-start | bytes 1048576 | tf_op jit(solution)/shard_map/all_to_all | solution.py:94
  75.0 1.4 %copy-start.3 = (s32[2]{0:T(128)S(1)}, s32[2]{0:T(128)}, u32[]{:S(2)}) copy-start(s32[2]{0:T(128)} %param.11) | copy-start | bytes 28
  76.9 6.1 %collective-permute-start.2 = (f32[2,2,1,4096]{3,2,1,0:T(1,128)S(1)}, f32[2,2,1,4096]{3,2,1,0:T(1,128)S(1)}, u32[]{:S(2)}, u32[]{:S(2)}) collective-permute-start(f32[2,2,1,4096]{3,2,1,0:T(1,128)S(1)} %get-tuple-element.25), channel_id=1, source_target_pairs={{0,1},{1,2},{2,3},{4,5},{5,6},{6,7},{8,9},{9,10},{10,11},{12,13},{... | collective-permute-start | bytes 196616 | tf_op jit(solution)/shard_map/ppermute | solution.py:20
  81.0 5.6 %collective-permute-start.3 = (f32[2,2,1,4096]{3,2,1,0:T(1,128)S(1)}, f32[2,2,1,4096]{3,2,1,0:T(1,128)S(1)}, u32[]{:S(2)}, u32[]{:S(2)}) collective-permute-start(f32[2,2,1,4096]{3,2,1,0:T(1,128)S(1)} %get-tuple-element.26), channel_id=1, source_target_pairs={{1,0},{2,1},{3,2},{5,4},{6,5},{7,6},{9,8},{10,9},{11,10},{13,12},{... | collective-permute-start | bytes 196616 | tf_op jit(solution)/shard_map/ppermute | solution.py:23
  88.3 4.4 %collective-permute-start.4 = (f32[2,2,1,4096]{3,2,1,0:T(1,128)S(1)}, f32[2,2,1,4096]{3,2,1,0:T(1,128)S(1)}, u32[]{:S(2)}, u32[]{:S(2)}) collective-permute-start(f32[2,2,1,4096]{3,2,1,0:T(1,128)S(1)} %get-tuple-element.23), channel_id=1, source_target_pairs={{0,1},{1,2},{2,3},{4,5},{5,6},{6,7},{8,9},{9,10},{10,11},{12,13},{... | collective-permute-start | bytes 196616 | tf_op jit(solution)/shard_map/ppermute | solution.py:20
  90.2 5.6 %collective-permute-start.5 = (f32[2,2,1,4096]{3,2,1,0:T(1,128)S(1)}, f32[2,2,1,4096]{3,2,1,0:T(1,128)S(1)}, u32[]{:S(2)}, u32[]{:S(2)}) collective-permute-start(f32[2,2,1,4096]{3,2,1,0:T(1,128)S(1)} %get-tuple-element.24), channel_id=1, source_target_pairs={{1,0},{2,1},{3,2},{5,4},{6,5},{7,6},{9,8},{10,9},{11,10},{13,12},{... | collective-permute-start | bytes 196616 | tf_op jit(solution)/shard_map/ppermute | solution.py:23
  97.4 4.6 %collective-permute-start.6 = (f32[2,2,1,4096]{3,2,1,0:T(1,128)S(1)}, f32[2,2,1,4096]{3,2,1,0:T(1,128)S(1)}, u32[]{:S(2)}, u32[]{:S(2)}) collective-permute-start(f32[2,2,1,4096]{3,2,1,0:T(1,128)S(1)} %get-tuple-element.21), channel_id=1, source_target_pairs={{0,1},{1,2},{2,3},{4,5},{5,6},{6,7},{8,9},{9,10},{10,11},{12,13},{... | collective-permute-start | bytes 196616 | tf_op jit(solution)/shard_map/ppermute | solution.py:20
  99.4 5.6 %collective-permute-start.7 = (f32[2,2,1,4096]{3,2,1,0:T(1,128)S(1)}, f32[2,2,1,4096]{3,2,1,0:T(1,128)S(1)}, u32[]{:S(2)}, u32[]{:S(2)}) collective-permute-start(f32[2,2,1,4096]{3,2,1,0:T(1,128)S(1)} %get-tuple-element.22), channel_id=1, source_target_pairs={{1,0},{2,1},{3,2},{5,4},{6,5},{7,6},{9,8},{10,9},{11,10},{13,12},{... | collective-permute-start | bytes 196616 | tf_op jit(solution)/shard_map/ppermute | solution.py:23
  106.6 4.4 %collective-permute-start.8 = (f32[2,2,1,4096]{3,2,1,0:T(1,128)S(1)}, f32[2,2,1,4096]{3,2,1,0:T(1,128)S(1)}, u32[]{:S(2)}, u32[]{:S(2)}) collective-permute-start(f32[2,2,1,4096]{3,2,1,0:T(1,128)S(1)} %get-tuple-element.19), channel_id=1, source_target_pairs={{0,1},{1,2},{2,3},{4,5},{5,6},{6,7},{8,9},{9,10},{10,11},{12,13},{... | collective-permute-start | bytes 196616 | tf_op jit(solution)/shard_map/ppermute | solution.py:20
  108.5 5.6 %collective-permute-start.9 = (f32[2,2,1,4096]{3,2,1,0:T(1,128)S(1)}, f32[2,2,1,4096]{3,2,1,0:T(1,128)S(1)}, u32[]{:S(2)}, u32[]{:S(2)}) collective-permute-start(f32[2,2,1,4096]{3,2,1,0:T(1,128)S(1)} %get-tuple-element.20), channel_id=1, source_target_pairs={{1,0},{2,1},{3,2},{5,4},{6,5},{7,6},{9,8},{10,9},{11,10},{13,12},{... | collective-permute-start | bytes 196616 | tf_op jit(solution)/shard_map/ppermute | solution.py:23
  115.7 4.4 %collective-permute-start.10 = (f32[2,2,1,4096]{3,2,1,0:T(1,128)S(1)}, f32[2,2,1,4096]{3,2,1,0:T(1,128)S(1)}, u32[]{:S(2)}, u32[]{:S(2)}) collective-permute-start(f32[2,2,1,4096]{3,2,1,0:T(1,128)S(1)} %get-tuple-element.17), channel_id=1, source_target_pairs={{0,1},{1,2},{2,3},{4,5},{5,6},{6,7},{8,9},{9,10},{10,11},{12,13},{... | collective-permute-start | bytes 196616 | tf_op jit(solution)/shard_map/ppermute | solution.py:20
  117.7 5.6 %collective-permute-start.11 = (f32[2,2,1,4096]{3,2,1,0:T(1,128)S(1)}, f32[2,2,1,4096]{3,2,1,0:T(1,128)S(1)}, u32[]{:S(2)}, u32[]{:S(2)}) collective-permute-start(f32[2,2,1,4096]{3,2,1,0:T(1,128)S(1)} %get-tuple-element.18), channel_id=1, source_target_pairs={{1,0},{2,1},{3,2},{5,4},{6,5},{7,6},{9,8},{10,9},{11,10},{13,12},{... | collective-permute-start | bytes 196616 | tf_op jit(solution)/shard_map/ppermute | solution.py:23
where the time goes:
time: 127 us; the launch traced here: 126 us
  waiting for transfers between devices  40.3 us (32%)
  starting transfers between devices  39.2 us (31%)
  local copies, waits for them, and re-layouts  31.7 us (25%)
  other arithmetic  12.7 us (10%)
  matrix products  1.43 us (1%)
    unnamed x13, local copies, waits for them, and re-layouts  20.1 us
    ppermute x6, starting transfers between devices, extended(): lax.ppermute(lax.slice_in_dim(block, block.shape[dim] - width, None, axis...  16.3 us
    ppermute x6, waiting for transfers between devices, extended(): lax.ppermute(lax.slice_in_dim(block, 0, width, axis=dim), axis, backward)  15.7 us
    ppermute x6, starting transfers between devices, extended(): lax.ppermute(lax.slice_in_dim(block, 0, width, axis=dim), axis, backward)  13.6 us
    all_to_all x1, waiting for transfers between devices, local(): lax.all_to_all(moved, 'sta', split_axis=1, concat_axis=3, tiled=True)  12.3 us
    all_to_all x1, waiting for transfers between devices, local(): lax.all_to_all(green_fields, 'sta', split_axis=3, concat_axis=1, tiled=True)  12.3 us
    all_to_all x1, local copies, waits for them, and re-layouts, local(): lax.all_to_all(green_fields, 'sta', split_axis=3, concat_axis=1, tiled=True)  8.9 us
    add x6, other arithmetic, relax(): near = lateral(inner, width_y) + padded[:, :, :-2] + padded[:, :, 2:]  6.88 us
  transfers between devices with their start and end apart: 14, of which 7 were waited for; matrix products, arithmetic and copies ran while one was open for 26% of the time, Pallas kernels for 0%

commit v1 on v0

v1 whole, which is shorter than its diff:
```python
import functools

import jax
import jax.numpy as jnp
from jax import lax
from jax.experimental import pallas as pl
from jax.experimental.pallas import tpu as pltpu
from jax.sharding import PartitionSpec as P

GY = 64
SWEEPS = 6
LANES = 128
HALO = 8
ROUNDS = 4

damping = 0.3
relaxation = 0.8
point_size = 2.0

MESH = pl.DeviceIdType.MESH
bf16 = jnp.bfloat16
f32 = jnp.float32


def partner(me, mask):
    other = me
    bit = 1
    while bit <= mask:
        if mask & bit:
            other = other + bit * (1 - 2 * ((me // bit) % 2))
        bit *= 2
    return other


def build_mixer(pairs_ref, values_ref, mixer, count, depth):
    number = pairs_ref.shape[0]
    eye = lax.broadcasted_iota(jnp.int32, (number, number), 0) == lax.broadcasted_iota(
        jnp.int32, (number, number), 1
    )
    pairs = pairs_ref[...]
    values = values_ref[...]
    columns = lax.broadcasted_iota(jnp.int32, (number, count), 1)
    rows = lax.broadcasted_iota(jnp.int32, (count, number), 0)

    def both(side):
        column = pairs[:, side : side + 1]
        row = jnp.sum(jnp.where(eye, column, 0), axis=0, keepdims=True)
        return (column == columns).astype(f32), (row == rows).astype(f32)

    first, first_t = both(0)
    second, second_t = both(1)
    parts = []
    for part, sign in ((0, 1.0), (1, -1.0)):
        weight = jnp.sum(jnp.where(eye, values[part : part + 1, :], 0.0), axis=1, keepdims=True)
        dot = functools.partial(
            jnp.dot, precision=lax.Precision.HIGHEST, preferred_element_type=f32
        )
        parts.append(
            (dot(first_t, weight * second) + sign * dot(second_t, weight * first)).astype(bf16)
        )
    size = count * depth
    block = min(size, 256)
    spread_t = (
        lax.broadcasted_iota(jnp.int32, (count, size), 1) // depth
        == lax.broadcasted_iota(jnp.int32, (count, size), 0)
    ).astype(bf16)
    for start in range(0, size, block):
        row_id = lax.broadcasted_iota(jnp.int32, (block, count), 0) + start
        spread = (row_id // depth == lax.broadcasted_iota(jnp.int32, (block, count), 1)).astype(
            bf16
        )
        same = (
            lax.broadcasted_iota(jnp.int32, (block, size), 0) % depth
            == lax.broadcasted_iota(jnp.int32, (block, size), 1) % depth
        )
        wide = []
        for part in parts:
            tall = jnp.dot(spread, part, preferred_element_type=f32).astype(bf16)
            full = jnp.dot(tall, spread_t, preferred_element_type=f32)
            wide.append(jnp.where(same, full, 0.0))
        here = slice(start, start + block)
        there = slice(size + start, size + start + block)
        mixer[here, :size] = wide[0].astype(bf16)
        mixer[here, size:] = (-wide[1]).astype(bf16)
        mixer[there, :size] = wide[1].astype(bf16)
        mixer[there, size:] = wide[0].astype(bf16)


def kernel(
    n,
    slabs,
    rounds,
    green,
    pairs_ref,
    values_ref,
    noise,
    wave,
    cell_ref,
    out,
    pieces,
    mixed,
    adjoint,
    mixer,
    edge_out,
    edge_in,
    map_in,
    source,
    scale_re,
    scale_im,
    field,
    send1,
    recv1,
    send2,
    recv2,
    send_edge,
    recv_edge,
    send_map,
    recv_map,
):
    me = lax.axis_index("sta")
    slab = lax.axis_index("slab")
    owned, depth, cells = green.shape[1], green.shape[2], green.shape[3]
    count = owned * n
    part = cells // rounds
    width = part // n
    tall = depth + 2 * HALO
    order = list(range(n - 1, 0, -1))
    above = slab + 1 < slabs
    below = slab > 0

    barrier = pltpu.get_barrier_semaphore()
    for mask in order:
        pl.semaphore_signal(
            barrier, inc=1, device_id={"sta": partner(me, mask)}, device_id_type=MESH
        )
    for step in (1, slabs - 1):
        pl.semaphore_signal(
            barrier, inc=1, device_id={"slab": lax.rem(slab + step, slabs)}, device_id_type=MESH
        )
    pl.semaphore_wait(barrier, n + 1)

    def lanes_of(turn, who):
        return pl.ds(pl.multiple_of(turn * part + who * width, width), width)

    def first_copy(turn, mask):
        other = partner(me, mask)
        return pltpu.make_async_remote_copy(
            src_ref=green.at[:, :, :, lanes_of(turn, other)],
            dst_ref=pieces.at[turn, :, pl.ds(me * owned, owned)],
            send_sem=send1.at[turn, mask],
            recv_sem=recv1.at[turn, mask],
            device_id={"sta": other},
            device_id_type=MESH,
        )

    def second_copy(turn, mask):
        other = partner(me, mask)
        return pltpu.make_async_remote_copy(
            src_ref=mixed.at[turn, :, pl.ds(other * owned, owned)],
            dst_ref=adjoint.at[:, :, :, lanes_of(turn, me)],
            send_sem=send2.at[turn, mask],
            recv_sem=recv2.at[turn, mask],
            device_id={"sta": other},
            device_id_type=MESH,
        )

    def map_copies(up):
        rows = slice(depth - HALO, depth) if up else slice(0, HALO)
        slot = 0 if up else 1
        target = slab + 1 if up else slab - 1
        return [
            pltpu.make_async_remote_copy(
                src_ref=ref.at[rows],
                dst_ref=map_in.at[slot, which],
                send_sem=send_map.at[slot, which],
                recv_sem=recv_map.at[slot, which],
                device_id={"slab": target},
                device_id_type=MESH,
            )
            for which, ref in enumerate((noise, wave))
        ]

    def edge_copy(up, turn):
        slot = 0 if up else 1
        target = slab + 1 if up else slab - 1
        here = slice(turn * part, (turn + 1) * part)
        return pltpu.make_async_remote_copy(
            src_ref=edge_out.at[slot, :, :, here],
            dst_ref=edge_in.at[slot, :, :, here],
            send_sem=send_edge.at[slot, turn],
            recv_sem=recv_edge.at[slot, turn],
            device_id={"slab": target},
            device_id_type=MESH,
        )

    def each(make, action):
        @pl.when(above)
        def _():
            action(make(True), make(False), True)

        @pl.when(below)
        def _():
            action(make(False), make(True), False)

    for turn in range(rounds):
        for mask in order:
            first_copy(turn, mask).start()

    def start_maps(mine, theirs, up):
        for copy in mine:
            copy.start()

    each(map_copies, start_maps)

    for turn in range(rounds):
        pieces[turn, :, pl.ds(me * owned, owned)] = green[:, :, :, lanes_of(turn, me)]
    build_mixer(pairs_ref, values_ref, mixer, count, depth)

    def wait_maps(mine, theirs, up):
        for copy in mine:
            copy.wait_send()
        for copy in theirs:
            copy.wait_recv()

    each(map_copies, wait_maps)

    def tile_of(t):
        return pl.ds(pl.multiple_of(t * LANES, LANES), LANES)

    def extend(low, middle, high):
        return jnp.concatenate([jnp.where(below, low, 0.0), middle, jnp.where(above, high, 0.0)], 0)

    def scales(t, carry):
        tile = tile_of(t)
        inside = extend(
            jnp.ones((HALO, LANES), f32), jnp.ones((depth, LANES), f32), jnp.ones((HALO, LANES), f32)
        )
        square = extend(map_in[0, 1, :, tile], wave[:, tile], map_in[1, 1, :, tile])
        diag = 6.0 - square
        lossy = damping * square
        factor = inside * relaxation / (diag * diag + lossy * lossy)
        scale_re[:, tile] = diag * factor
        scale_im[:, tile] = lossy * factor
        return carry

    lax.fori_loop(0, cells // LANES, scales, 0)
    for buffer in range(2):
        for k in range(2 * owned):
            field[buffer, k, :, :LANES] = jnp.zeros((tall, LANES), f32)
            field[buffer, k, :, LANES + cells :] = jnp.zeros((tall, LANES), f32)

    size = 2 * count * depth
    block = min(size, 256)
    for turn in range(rounds):
        for mask in order:
            first_copy(turn, mask).wait_recv()
        stacked = pieces[turn].reshape(size, width)
        for start in range(0, size, block):
            product = jnp.dot(
                mixer[start : start + block, :], stacked, preferred_element_type=f32
            ).astype(bf16)
            side = start // (count * depth)
            station = (start % (count * depth)) // depth
            mixed[turn, side, station : station + block // depth] = product.reshape(
                block // depth, depth, width
            )
        for mask in order:
            second_copy(turn, mask).start()
        adjoint[:, :, :, lanes_of(turn, me)] = mixed[turn, :, pl.ds(me * owned, owned)]

    columns = lax.broadcasted_iota(jnp.int32, (1, LANES), 1)
    not_first = (columns % GY) != 0
    not_last = (columns % GY) != GY - 1
    upper_half = columns >= GY
    per_part = part // LANES

    def pack(t, carry):
        tile = tile_of(t)
        for k in range(owned):
            re = adjoint[0, k, :, tile].astype(f32)
            im = adjoint[1, k, :, tile].astype(f32)
            edge_out[0, k, :, tile] = jnp.concatenate(
                [re[depth - HALO :], im[depth - HALO :]], 0
            ).astype(bf16)
            edge_out[1, k, :, tile] = jnp.concatenate([re[:HALO], im[:HALO]], 0).astype(bf16)
        return carry

    spot_rows = (
        (slab * depth - HALO + lax.broadcasted_iota(jnp.int32, (tall, LANES), 0)) * cells
        + lax.broadcasted_iota(jnp.int32, (tall, LANES), 1)
    )

    def begin(t, carry):
        tile = tile_of(t)
        shifted = tile_of(t + 1)
        power = extend(map_in[0, 0, :, tile], noise[:, tile], map_in[1, 0, :, tile])
        s_re = scale_re[:, tile]
        s_im = scale_im[:, tile]
        ids = spot_rows + t * LANES
        for k in range(owned):
            low = edge_in[0, k, :, tile].astype(f32)
            high = edge_in[1, k, :, tile].astype(f32)
            re = extend(low[:HALO], adjoint[0, k, :, tile].astype(f32), high[:HALO])
            im = extend(low[HALO:], adjoint[1, k, :, tile].astype(f32), high[HALO:])
            re = power * re + jnp.where(ids == cell_ref[k], point_size, 0.0)
            im = power * im
            source[2 * k, :, tile] = re
            source[2 * k + 1, :, tile] = im
            field[0, 2 * k, :, shifted] = s_re * re - s_im * im
            field[0, 2 * k + 1, :, shifted] = s_re * im + s_im * re
        return carry

    def near(old, k, t):
        v = field[old, k, :, tile_of(t + 1)]
        before = field[old, k, :, tile_of(t)]
        after = field[old, k, :, tile_of(t + 2)]
        along_x = pltpu.roll(v + jnp.where(upper_half, before, after), GY, 1)
        left = jnp.where(not_first, pltpu.roll(v, 1, 1), 0.0)
        right = jnp.where(not_last, pltpu.roll(v, LANES - 1, 1), 0.0)
        along_z = pltpu.roll(v, 1, 0) + pltpu.roll(v, tall - 1, 0)
        return v, along_x + left + right + along_z

    kept = 1.0 - relaxation

    def sweep(old, final, t, carry):
        tile = tile_of(t)
        s_re = scale_re[:, tile]
        s_im = scale_im[:, tile]
        for k in range(owned):
            v_re, n_re = near(old, 2 * k, t)
            v_im, n_im = near(old, 2 * k + 1, t)
            n_re = n_re + source[2 * k, :, tile]
            n_im = n_im + source[2 * k + 1, :, tile]
            re = kept * v_re + (s_re * n_re - s_im * n_im)
            im = kept * v_im + (s_re * n_im + s_im * n_re)
            if final:
                out[0, k, :, tile] = re[HALO : HALO + depth]
                out[1, k, :, tile] = im[HALO : HALO + depth]
            else:
                field[1 - old, 2 * k, :, tile_of(t + 1)] = re
                field[1 - old, 2 * k + 1, :, tile_of(t + 1)] = im
        return carry

    def compute(turn):
        def wait_edge(mine, theirs, up):
            theirs.wait_recv()

        each(lambda up: edge_copy(up, turn), wait_edge)
        lax.fori_loop(turn * per_part, (turn + 1) * per_part, begin, 0)
        for number in range(1, SWEEPS):
            low = 0 if turn == 0 else max(turn * per_part - number, 0)
            high = cells // LANES if turn == rounds - 1 else max((turn + 1) * per_part - number, 0)
            if high > low:
                old = (number - 1) % 2
                lax.fori_loop(
                    low, high, functools.partial(sweep, old, number == SWEEPS - 1), 0
                )

    for turn in range(rounds):
        for mask in order:
            second_copy(turn, mask).wait_recv()
        lax.fori_loop(turn * per_part, (turn + 1) * per_part, pack, 0)

        def start_edge(mine, theirs, up):
            mine.start()

        each(lambda up: edge_copy(up, turn), start_edge)
        if turn > 0:
            compute(turn - 1)
    compute(rounds - 1)

    for turn in range(rounds):
        for mask in order:
            first_copy(turn, mask).wait_send()
            second_copy(turn, mask).wait_send()

        def end_edge(mine, theirs, up):
            mine.wait_send()

        each(lambda up: edge_copy(up, turn), end_edge)


def local(n, slabs, green_fields, pair_list, pair_values, noise_map, wave_square, station_cell):
    _, owned, depth, cells = green_fields.shape
    count = owned * n
    rounds = min(ROUNDS, cells // (n * LANES))
    width = cells // (n * rounds)
    tall = depth + 2 * HALO
    size = 2 * count * depth
    vmem = pl.BlockSpec(memory_space=pltpu.VMEM)
    dma = pltpu.SemaphoreType.DMA
    return pl.pallas_call(
        functools.partial(kernel, n, slabs, rounds),
        out_shape=jax.ShapeDtypeStruct((2, owned, depth, cells), f32),
        in_specs=[vmem] * 5 + [pl.BlockSpec(memory_space=pltpu.SMEM)],
        out_specs=vmem,
        scratch_shapes=[
            pltpu.VMEM((rounds, 2, count, depth, width), bf16),
            pltpu.VMEM((rounds, 2, count, depth, width), bf16),
            pltpu.VMEM((2, owned, depth, cells), bf16),
            pltpu.VMEM((size, size), bf16),
            pltpu.VMEM((2, owned, 2 * HALO, cells), bf16),
            pltpu.VMEM((2, owned, 2 * HALO, cells), bf16),
            pltpu.VMEM((2, 2, HALO, cells), f32),
            pltpu.VMEM((2 * owned, tall, cells), f32),
            pltpu.VMEM((tall, cells), f32),
            pltpu.VMEM((tall, cells), f32),
            pltpu.VMEM((2, 2 * owned, tall, cells + 2 * LANES), f32),
            dma((rounds, n)),
            dma((rounds, n)),
            dma((rounds, n)),
            dma((rounds, n)),
            dma((2, rounds)),
            dma((2, rounds)),
            dma((2, 2)),
            dma((2, 2)),
        ],
        compiler_params=pltpu.CompilerParams(
            collective_id=0, has_side_effects=True, vmem_limit_bytes=48 * 1024 * 1024
        ),
    )(green_fields, pair_list, pair_values, noise_map, wave_square, station_cell)


def solution(mesh):
    placed = (P(None, "sta", "slab", None), P(), P(), P("slab", None), P("slab", None), P("sta"))
    return jax.shard_map(
        functools.partial(local, mesh.shape["sta"], mesh.shape["slab"]),
        mesh=mesh,
        in_specs=placed,
        out_specs=P(None, "sta", "slab", None),
        check_vma=False,
    )
```

time: 127 us -> 63 us (0.50)
  Pallas kernels: 0 us -> 58 us
  waiting for transfers between devices: 40.3 us -> 0 us
  starting transfers between devices: 39.2 us -> 0 us
  local copies, waits for them, and re-layouts: 31.7 us -> 4.71 us
  other arithmetic: 12.7 us -> 0 us
  matrix products: 1.43 us -> 0 us
    pallas_call x0 -> x1, Pallas kernels: none -> 58 us  [local(): pl.pallas_call(functools.partial(kernel, n, slabs, rounds), out_shape=jax...]
    ppermute x12 -> x0, starting transfers between devices: 30 us -> none  [the longest x6 16.3 us: extended(): lax.ppermute(lax.slice_in_dim(block, block.shape[dim] - width, None, axis...]
    all_to_all x2 -> x0, waiting for transfers between devices: 24.6 us -> none  [the longest x1 12.3 us: local(): lax.all_to_all(moved, 'sta', split_axis=1, concat_axis=3, tiled=True)]
    ppermute x12 -> x0, waiting for transfers between devices: 15.7 us -> none  [the longest x6 15.7 us: extended(): lax.ppermute(lax.slice_in_dim(block, 0, width, axis=dim), axis, backward)]
    unnamed x13 -> x12, local copies, waits for them, and re-layouts: 20.1 us -> 4.71 us
    all_to_all x2 -> x0, starting transfers between devices: 9.21 us -> none  [the longest x1 5.66 us: local(): lax.all_to_all(green_fields, 'sta', split_axis=3, concat_axis=1, tiled=True)]
    all_to_all x1 -> x0, local copies, waits for them, and re-layouts: 8.9 us -> none  [local(): lax.all_to_all(green_fields, 'sta', split_axis=3, concat_axis=1, tiled=True)]
    add x8 -> x0, other arithmetic: 7.08 us -> none  [the longest x6 6.88 us: relax(): near = lateral(inner, width_y) + padded[:, :, :-2] + padded[:, :, 2:]]
  transfers between devices with their start and end apart: 14 -> 0, of which waited for: 7 -> 0; matrix products, arithmetic and copies ran while one was open for 26% -> 0% of each run, Pallas kernels for 0% -> 0%
where the time goes in v1:
time: 63 us; the launch traced here: 62.8 us
  Pallas kernels  58 us (92%)
  local copies, waits for them, and re-layouts  4.71 us (7%)
    pallas_call x1, Pallas kernels, local(): pl.pallas_call(functools.partial(kernel, n, slabs, rounds), out_shape=jax...  58 us
    unnamed x12, local copies, waits for them, and re-layouts  4.71 us

profile of v1, /device:TPU:1, one launch (start us, length us, event | category | flops | bytes accessed | tf_op | source)
XLA Modules:
  0.0 62.8 jit_solution(12034022804975879331)
XLA Ops:
  0.0 0.0 copy-start.4
  0.0 0.0 copy-start.3
  0.0 0.8 %copy.7.pairs_ref = s32[64,2]{1,0:T(8,128)S(1)} copy(s32[64,2]{0,1:T(2,128)} %param.7) | data formatting | bytes 1024 | tf_op args[1]
  0.8 0.0 copy-done.4
  0.8 0.0 copy-done.3
  0.8 0.0 copy-start
  0.8 1.0 %copy-done = bf16[2,2,16,4096]{3,2,1,0:T(8,128)(2,1)S(1)} copy-done((bf16[2,2,16,4096]{3,2,1,0:T(8,128)(2,1)S(1)}, bf16[2,2,16,4096]{3,2,1,0:T(8,128)(2,1)}, u32[]{:S(2)}) %copy-start) | copy-done | bytes 524312
  1.9 0.0 copy-start.1
  1.9 0.9 %copy-done.1 = f32[16,4096]{1,0:T(8,128)S(1)} copy-done((f32[16,4096]{1,0:T(8,128)S(1)}, f32[16,4096]{1,0:T(8,128)}, u32[]{:S(2)}) %copy-start.1) | copy-done | bytes 262168
  2.8 0.0 copy-start.2
  2.8 0.9 %copy-done.2 = f32[16,4096]{1,0:T(8,128)S(1)} copy-done((f32[16,4096]{1,0:T(8,128)S(1)}, f32[16,4096]{1,0:T(8,128)}, u32[]{:S(2)}) %copy-start.2) | copy-done | bytes 262168
  3.8 58.0 %shard_map.64 = f32[2,2,16,4096]{3,2,1,0:T(8,128)S(1)} custom-call(bf16[2,2,16,4096]{3,2,1,0:T(8,128)(2,1)S(1)} %copy-done, s32[64,2]{1,0:T(8,128)S(1)} %copy.7.pairs_ref, f32[2,64]{1,0:T(2,128)S(1)} %copy-done.3, f32[16,4096]{1,0:T(8,128)S(1)} %copy-done.1, f32[16,4096]{1,0:T(8,128)S(1)} %copy-done.2, s32[2]{0:T(128)S(1)} %copy-done.4), custom_call_target="tpu_custom_call" | custom-call | tf_op jit(solution)/shard_map/pallas_call | solution.py:392
  61.8 1.0 %copy.9 = f32[2,2,16,4096]{3,2,1,0:T(8,128)} copy(f32[2,2,16,4096]{3,2,1,0:T(8,128)S(1)} %shard_map.64) | data formatting | bytes 2097152
Async XLA Ops:
  0.0 0.8 %copy-start.4 = (s32[2]{0:T(128)S(1)}, s32[2]{0:T(128)}, u32[]{:S(2)}) copy-start(s32[2]{0:T(128)} %cell_ref.1) | copy-start | bytes 28
  0.0 0.8 %copy-start.3 = (f32[2,64]{1,0:T(2,128)S(1)}, f32[2,64]{1,0:T(2,128)}, u32[]{:S(2)}) copy-start(f32[2,64]{1,0:T(2,128)} %values_ref.1) | copy-start | bytes 1540
  0.8 1.0 %copy-start = (bf16[2,2,16,4096]{3,2,1,0:T(8,128)(2,1)S(1)}, bf16[2,2,16,4096]{3,2,1,0:T(8,128)(2,1)}, u32[]{:S(2)}) copy-start(bf16[2,2,16,4096]{3,2,1,0:T(8,128)(2,1)} %green.1) | copy-start | bytes 1572868
  1.9 0.9 %copy-start.1 = (f32[16,4096]{1,0:T(8,128)S(1)}, f32[16,4096]{1,0:T(8,128)}, u32[]{:S(2)}) copy-start(f32[16,4096]{1,0:T(8,128)} %noise.1) | copy-start | bytes 786436
  2.8 0.9 %copy-start.2 = (f32[16,4096]{1,0:T(8,128)S(1)}, f32[16,4096]{1,0:T(8,128)}, u32[]{:S(2)}) copy-start(f32[16,4096]{1,0:T(8,128)} %wave.1) | copy-start | bytes 786436

commit v2 on v1

--- a/solution.py
+++ b/solution.py
@@ -12,6 +12,7 @@
 LANES = 128
 HALO = 8
 ROUNDS = 4
+GROUP = 2
 
 damping = 0.3
 relaxation = 0.8
@@ -33,7 +34,7 @@
 
 
 def build_mixer(pairs_ref, values_ref, mixer, count, depth):
-    number = pairs_ref.shape[0]
+    number = pairs_ref.shape[1]
     eye = lax.broadcasted_iota(jnp.int32, (number, number), 0) == lax.broadcasted_iota(
         jnp.int32, (number, number), 1
     )
@@ -43,8 +44,8 @@
     rows = lax.broadcasted_iota(jnp.int32, (count, number), 0)
 
     def both(side):
-        column = pairs[:, side : side + 1]
-        row = jnp.sum(jnp.where(eye, column, 0), axis=0, keepdims=True)
+        row = pairs[side : side + 1, :]
+        column = jnp.sum(jnp.where(eye, row, 0), axis=1, keepdims=True)
         return (column == columns).astype(f32), (row == rows).astype(f32)
 
     first, first_t = both(0)
@@ -93,10 +94,12 @@
     green,
     pairs_ref,
     values_ref,
+    noise_hbm,
+    wave_hbm,
+    cell_ref,
+    out,
     noise,
     wave,
-    cell_ref,
-    out,
     pieces,
     mixed,
     adjoint,
@@ -105,9 +108,12 @@
     edge_in,
     map_in,
     source,
+    source_edge,
     scale_re,
     scale_im,
-    field,
+    map_scale,
+    field_a,
+    field_b,
     send1,
     recv1,
     send2,
@@ -116,6 +122,8 @@
     recv_edge,
     send_map,
     recv_map,
+    own_sem,
+    local_sem,
 ):
     me = lax.axis_index("sta")
     slab = lax.axis_index("slab")
@@ -123,11 +131,17 @@
     count = owned * n
     part = cells // rounds
     width = part // n
-    tall = depth + 2 * HALO
+    tall = depth + HALO
+    half = HALO // 2
+    fields = (field_a, field_b)
     order = list(range(n - 1, 0, -1))
     above = slab + 1 < slabs
     below = slab > 0
 
+    local_maps = [
+        pltpu.make_async_copy(noise_hbm, noise, local_sem.at[0]),
+        pltpu.make_async_copy(wave_hbm, wave, local_sem.at[1]),
+    ]
     barrier = pltpu.get_barrier_semaphore()
     for mask in order:
         pl.semaphore_signal(
@@ -177,7 +191,7 @@
                 device_id={"slab": target},
                 device_id_type=MESH,
             )
-            for which, ref in enumerate((noise, wave))
+            for which, ref in enumerate((noise_hbm, wave_hbm))
         ]
 
     def edge_copy(up, turn):
@@ -212,8 +226,16 @@
 
     each(map_copies, start_maps)
 
-    for turn in range(rounds):
-        pieces[turn, :, pl.ds(me * owned, owned)] = green[:, :, :, lanes_of(turn, me)]
+    own = [
+        pltpu.make_async_copy(
+            green.at[:, :, :, lanes_of(turn, me)],
+            pieces.at[turn, :, pl.ds(me * owned, owned)],
+            own_sem.at[turn],
+        )
+        for turn in range(rounds)
+    ]
+    for copy in own + local_maps:
+        copy.start()
     build_mixer(pairs_ref, values_ref, mixer, count, depth)
 
     def wait_maps(mine, theirs, up):
@@ -223,35 +245,48 @@
             copy.wait_recv()
 
     each(map_copies, wait_maps)
+    for copy in local_maps:
+        copy.wait()
 
     def tile_of(t):
         return pl.ds(pl.multiple_of(t * LANES, LANES), LANES)
 
-    def extend(low, middle, high):
-        return jnp.concatenate([jnp.where(below, low, 0.0), middle, jnp.where(above, high, 0.0)], 0)
+    def scale_of(square):
+        diag = 6.0 - square
+        lossy = damping * square
+        factor = relaxation / (diag * diag + lossy * lossy)
+        return diag * factor, lossy * factor
+
+    edge_rows = lax.broadcasted_iota(jnp.int32, (HALO, LANES), 0)
+    is_high = edge_rows < half
 
     def scales(t, carry):
         tile = tile_of(t)
-        inside = extend(
-            jnp.ones((HALO, LANES), f32), jnp.ones((depth, LANES), f32), jnp.ones((HALO, LANES), f32)
-        )
-        square = extend(map_in[0, 1, :, tile], wave[:, tile], map_in[1, 1, :, tile])
-        diag = 6.0 - square
-        lossy = damping * square
-        factor = inside * relaxation / (diag * diag + lossy * lossy)
-        scale_re[:, tile] = diag * factor
-        scale_im[:, tile] = lossy * factor
+        s_re, s_im = scale_of(wave[:, tile])
+        scale_re[:depth, tile] = s_re
+        scale_im[:depth, tile] = s_im
+        for slot, there in ((0, below), (1, above)):
+            l_re, l_im = scale_of(jnp.where(there, map_in[slot, 1, :, tile], 0.0))
+            map_scale[slot, 0, :, tile] = jnp.where(there, l_re, 0.0)
+            map_scale[slot, 1, :, tile] = jnp.where(there, l_im, 0.0)
+        scale_re[depth:, tile] = jnp.where(
+            is_high, map_scale[1, 0, :, tile], map_scale[0, 0, :, tile]
+        )
+        scale_im[depth:, tile] = jnp.where(
+            is_high, map_scale[1, 1, :, tile], map_scale[0, 1, :, tile]
+        )
         return carry
 
     lax.fori_loop(0, cells // LANES, scales, 0)
-    for buffer in range(2):
+    for ref in fields:
         for k in range(2 * owned):
-            field[buffer, k, :, :LANES] = jnp.zeros((tall, LANES), f32)
-            field[buffer, k, :, LANES + cells :] = jnp.zeros((tall, LANES), f32)
+            ref[k, :, :LANES] = jnp.zeros((tall, LANES), f32)
+            ref[k, :, LANES + cells :] = jnp.zeros((tall, LANES), f32)
 
     size = 2 * count * depth
     block = min(size, 256)
     for turn in range(rounds):
+        own[turn].wait()
         for mask in order:
             first_copy(turn, mask).wait_recv()
         stacked = pieces[turn].reshape(size, width)
@@ -274,7 +309,7 @@
     upper_half = columns >= GY
     per_part = part // LANES
 
-    def pack(t, carry):
+    def pack(t):
         tile = tile_of(t)
         for k in range(owned):
             re = adjoint[0, k, :, tile].astype(f32)
@@ -283,37 +318,68 @@
                 [re[depth - HALO :], im[depth - HALO :]], 0
             ).astype(bf16)
             edge_out[1, k, :, tile] = jnp.concatenate([re[:HALO], im[:HALO]], 0).astype(bf16)
-        return carry
-
-    spot_rows = (
-        (slab * depth - HALO + lax.broadcasted_iota(jnp.int32, (tall, LANES), 0)) * cells
-        + lax.broadcasted_iota(jnp.int32, (tall, LANES), 1)
-    )
-
-    def begin(t, carry):
+
+    def ids_from(row, rows):
+        return (slab * depth + row + lax.broadcasted_iota(jnp.int32, (rows, LANES), 0)) * cells + (
+            lax.broadcasted_iota(jnp.int32, (rows, LANES), 1)
+        )
+
+    ids_main = ids_from(0, depth)
+    ids_low = ids_from(-HALO, HALO)
+    ids_high = ids_from(depth, HALO)
+
+    def begin(t):
         tile = tile_of(t)
         shifted = tile_of(t + 1)
-        power = extend(map_in[0, 0, :, tile], noise[:, tile], map_in[1, 0, :, tile])
-        s_re = scale_re[:, tile]
-        s_im = scale_im[:, tile]
-        ids = spot_rows + t * LANES
+        step = t * LANES
         for k in range(owned):
             low = edge_in[0, k, :, tile].astype(f32)
             high = edge_in[1, k, :, tile].astype(f32)
-            re = extend(low[:HALO], adjoint[0, k, :, tile].astype(f32), high[:HALO])
-            im = extend(low[HALO:], adjoint[1, k, :, tile].astype(f32), high[HALO:])
-            re = power * re + jnp.where(ids == cell_ref[k], point_size, 0.0)
-            im = power * im
-            source[2 * k, :, tile] = re
-            source[2 * k + 1, :, tile] = im
-            field[0, 2 * k, :, shifted] = s_re * re - s_im * im
-            field[0, 2 * k + 1, :, shifted] = s_re * im + s_im * re
-        return carry
+
+            def start(power, re, im, ids, s_re, s_im):
+                re = power * re + jnp.where(ids + step == cell_ref[k], point_size, 0.0)
+                im = power * im
+                return re, im, s_re * re - s_im * im, s_re * im + s_im * re
+
+            def outer(slot, there, values, ids):
+                return start(
+                    jnp.where(there, map_in[slot, 0, :, tile], 0.0),
+                    jnp.where(there, values[:HALO], 0.0),
+                    jnp.where(there, values[HALO:], 0.0),
+                    ids,
+                    map_scale[slot, 0, :, tile],
+                    map_scale[slot, 1, :, tile],
+                )
+
+            main = start(
+                noise[:, tile],
+                adjoint[0, k, :, tile].astype(f32),
+                adjoint[1, k, :, tile].astype(f32),
+                ids_main,
+                scale_re[:depth, tile],
+                scale_im[:depth, tile],
+            )
+            under = outer(0, below, low, ids_low)
+            over = outer(1, above, high, ids_high)
+            for c in range(2):
+                kc = 2 * k + c
+                source[kc, :depth, tile] = main[c]
+                edge = jnp.where(is_high, over[c], under[c])
+                source[kc, depth:, tile] = edge
+                fields[0][kc, :depth, shifted] = main[2 + c]
+                f_over, f_under = over[2 + c], under[2 + c]
+                fields[0][kc, depth:, shifted] = jnp.where(is_high, f_over, f_under)
+                fifth_over = pltpu.roll(f_over, HALO - 1, 0) - pltpu.roll(f_under, HALO - 1, 0)
+                fifth_under = pltpu.roll(f_under, 1, 0) - pltpu.roll(f_over, 1, 0)
+                fix = jnp.where(edge_rows == half - 1, fifth_over, 0.0) + jnp.where(
+                    edge_rows == half, fifth_under, 0.0
+                )
+                source_edge[kc, :, tile] = edge + fix
 
     def near(old, k, t):
-        v = field[old, k, :, tile_of(t + 1)]
-        before = field[old, k, :, tile_of(t)]
-        after = field[old, k, :, tile_of(t + 2)]
+        v = fields[old][k, :, tile_of(t + 1)]
+        before = fields[old][k, :, tile_of(t)]
+        after = fields[old][k, :, tile_of(t + 2)]
         along_x = pltpu.roll(v + jnp.where(upper_half, before, after), GY, 1)
         left = jnp.where(not_first, pltpu.roll(v, 1, 1), 0.0)
         right = jnp.where(not_last, pltpu.roll(v, LANES - 1, 1), 0.0)
@@ -322,44 +388,63 @@
 
     kept = 1.0 - relaxation
 
-    def sweep(old, final, t, carry):
+    def sweep(number, t):
+        old = (number - 1) % 2
+        final = number == SWEEPS - 1
+        rows = depth if final else tall
         tile = tile_of(t)
-        s_re = scale_re[:, tile]
-        s_im = scale_im[:, tile]
+        s_re = scale_re[:rows, tile]
+        s_im = scale_im[:rows, tile]
+
+        def pulled(kc):
+            v, n = near(old, kc, t)
+            if number == 1:
+                added = jnp.concatenate([source[kc, :depth, tile], source_edge[kc, :, tile]], 0)
+            else:
+                added = source[kc, :rows, tile]
+            return v[:rows], n[:rows] + added
+
         for k in range(owned):
-            v_re, n_re = near(old, 2 * k, t)
-            v_im, n_im = near(old, 2 * k + 1, t)
-            n_re = n_re + source[2 * k, :, tile]
-            n_im = n_im + source[2 * k + 1, :, tile]
+            v_re, n_re = pulled(2 * k)
+            v_im, n_im = pulled(2 * k + 1)
             re = kept * v_re + (s_re * n_re - s_im * n_im)
             im = kept * v_im + (s_re * n_im + s_im * n_re)
             if final:
-                out[0, k, :, tile] = re[HALO : HALO + depth]
-                out[1, k, :, tile] = im[HALO : HALO + depth]
+                out[0, k, :, tile] = re
+                out[1, k, :, tile] = im
             else:
-                field[1 - old, 2 * k, :, tile_of(t + 1)] = re
-                field[1 - old, 2 * k + 1, :, tile_of(t + 1)] = im
-        return carry
+                fields[1 - old][2 * k, :, tile_of(t + 1)] = re
+                fields[1 - old][2 * k + 1, :, tile_of(t + 1)] = im
+
+    def run(low, high, work):
+        groups = (high - low) // GROUP
+
+        def many(g, carry):
+            for j in range(GROUP):
+                work(low + g * GROUP + j)
+            return carry
+
+        if groups:
+            lax.fori_loop(0, groups, many, 0)
+        for t in range(low + groups * GROUP, high):
+            work(t)
 
     def compute(turn):
         def wait_edge(mine, theirs, up):
             theirs.wait_recv()
 
         each(lambda up: edge_copy(up, turn), wait_edge)
-        lax.fori_loop(turn * per_part, (turn + 1) * per_part, begin, 0)
+        run(turn * per_part, (turn + 1) * per_part, begin)
         for number in range(1, SWEEPS):
             low = 0 if turn == 0 else max(turn * per_part - number, 0)
             high = cells // LANES if turn == rounds - 1 else max((turn + 1) * per_part - number, 0)
             if high > low:
-                old = (number - 1) % 2
-                lax.fori_loop(
-                    low, high, functools.partial(sweep, old, number == SWEEPS - 1), 0
-                )
+                run(low, high, functools.partial(sweep, number))
 
     for turn in range(rounds):
         for mask in order:
             second_copy(turn, mask).wait_recv()
-        lax.fori_loop(turn * per_part, (turn + 1) * per_part, pack, 0)
+        run(turn * per_part, (turn + 1) * per_part, pack)
 
         def start_edge(mine, theirs, up):
             mine.start()
@@ -385,16 +470,19 @@
     count = owned * n
     rounds = min(ROUNDS, cells // (n * LANES))
     width = cells // (n * rounds)
-    tall = depth + 2 * HALO
+    tall = depth + HALO
     size = 2 * count * depth
     vmem = pl.BlockSpec(memory_space=pltpu.VMEM)
+    hbm = pl.BlockSpec(memory_space=pl.ANY)
     dma = pltpu.SemaphoreType.DMA
     return pl.pallas_call(
         functools.partial(kernel, n, slabs, rounds),
         out_shape=jax.ShapeDtypeStruct((2, owned, depth, cells), f32),
-        in_specs=[vmem] * 5 + [pl.BlockSpec(memory_space=pltpu.SMEM)],
+        in_specs=[hbm, vmem, vmem, hbm, hbm, pl.BlockSpec(memory_space=pltpu.SMEM)],
         out_specs=vmem,
         scratch_shapes=[
+            pltpu.VMEM((depth, cells), f32),
+            pltpu.VMEM((depth, cells), f32),
             pltpu.VMEM((rounds, 2, count, depth, width), bf16),
             pltpu.VMEM((rounds, 2, count, depth, width), bf16),
             pltpu.VMEM((2, owned, depth, cells), bf16),
@@ -403,9 +491,12 @@
             pltpu.VMEM((2, owned, 2 * HALO, cells), bf16),
             pltpu.VMEM((2, 2, HALO, cells), f32),
             pltpu.VMEM((2 * owned, tall, cells), f32),
+            pltpu.VMEM((2 * owned, HALO, cells), f32),
             pltpu.VMEM((tall, cells), f32),
             pltpu.VMEM((tall, cells), f32),
-            pltpu.VMEM((2, 2 * owned, tall, cells + 2 * LANES), f32),
+            pltpu.VMEM((2, 2, HALO, cells), f32),
+            pltpu.VMEM((2 * owned, tall, cells + 2 * LANES), f32),
+            pltpu.VMEM((2 * owned, tall, cells + 2 * LANES), f32),
             dma((rounds, n)),
             dma((rounds, n)),
             dma((rounds, n)),
@@ -414,11 +505,13 @@
             dma((2, rounds)),
             dma((2, 2)),
             dma((2, 2)),
+            dma((rounds,)),
+            dma((2,)),
         ],
         compiler_params=pltpu.CompilerParams(
             collective_id=0, has_side_effects=True, vmem_limit_bytes=48 * 1024 * 1024
         ),
-    )(green_fields, pair_list, pair_values, noise_map, wave_square, station_cell)
+    )(green_fields, pair_list.T, pair_values, noise_map, wave_square, station_cell)
 
 
 def solution(mesh):

time: 63 us -> 48.4 us (0.77)
  Pallas kernels: 58 us -> 42.9 us
    pallas_call x1, Pallas kernels: 58 us -> 42.9 us  [local(): pl.pallas_call(functools.partial(kernel, n, slabs, rounds), out_shape=jax...]
    unnamed x12 -> x13, local copies, waits for them, and re-layouts: 4.71 us -> 5.28 us
where the time goes in v2:
time: 48.4 us; the launch traced here: 48.2 us
  Pallas kernels  42.9 us (89%)
  local copies, waits for them, and re-layouts  5.28 us (11%)
    pallas_call x1, Pallas kernels, local(): pl.pallas_call(functools.partial(kernel, n, slabs, rounds), out_shape=jax...  42.9 us
    unnamed x13, local copies, waits for them, and re-layouts  5.28 us

profile of v2, /device:TPU:1, one launch (start us, length us, event | category | flops | bytes accessed | tf_op | source)
XLA Modules:
  0.0 48.2 jit_solution(12597455383941976922)
XLA Ops:
  0.0 0.0 copy-start.5
  0.0 0.0 copy-start.3
  0.0 0.7 %copy-done.5 = s32[2]{0:T(128)S(1)} copy-done((s32[2]{0:T(128)S(1)}, s32[2]{0:T(128)}, u32[]{:S(2)}) %copy-start.5) | copy-done | bytes 32
  0.7 0.0 copy-done.3
  0.7 0.0 copy-start
  0.7 1.0 %copy-done = bf16[2,2,16,4096]{3,2,1,0:T(8,128)(2,1)S(1)} copy-done((bf16[2,2,16,4096]{3,2,1,0:T(8,128)(2,1)S(1)}, bf16[2,2,16,4096]{3,2,1,0:T(8,128)(2,1)}, u32[]{:S(2)}) %copy-start) | copy-done | bytes 524312
  1.7 0.0 copy-start.1
  1.7 0.9 %copy-done.1 = f32[16,4096]{1,0:T(8,128)S(1)} copy-done((f32[16,4096]{1,0:T(8,128)S(1)}, f32[16,4096]{1,0:T(8,128)}, u32[]{:S(2)}) %copy-start.1) | copy-done | bytes 262168
  2.7 0.0 copy-start.2
  2.7 0.9 %copy-done.2 = f32[16,4096]{1,0:T(8,128)S(1)} copy-done((f32[16,4096]{1,0:T(8,128)S(1)}, f32[16,4096]{1,0:T(8,128)}, u32[]{:S(2)}) %copy-start.2) | copy-done | bytes 262168
  3.6 0.0 copy-start.4
  3.6 0.7 %copy-done.4 = f32[2,64]{1,0:T(2,128)S(1)} copy-done((f32[2,64]{1,0:T(2,128)S(1)}, f32[2,64]{1,0:T(2,128)}, u32[]{:S(2)}) %copy-start.4) | copy-done | bytes 536
  4.3 42.9 %shard_map.64 = f32[2,2,16,4096]{3,2,1,0:T(8,128)S(1)} custom-call(bf16[2,2,16,4096]{3,2,1,0:T(8,128)(2,1)S(1)} %copy-done, s32[2,64]{1,0:T(2,128)S(1)} %bitcast.1, f32[2,64]{1,0:T(2,128)S(1)} %copy-done.4, f32[16,4096]{1,0:T(8,128)S(1)} %copy-done.1, f32[16,4096]{1,0:T(8,128)S(1)} %copy-done.2, s32[2]{0:T(128)S(1)} %copy-done.5), custom_call_target="tpu_custom_call" | custom-call | tf_op jit(solution)/shard_map/pallas_call | solution.py:478
  47.2 1.0 %copy.8 = f32[2,2,16,4096]{3,2,1,0:T(8,128)} copy(f32[2,2,16,4096]{3,2,1,0:T(8,128)S(1)} %shard_map.64) | data formatting | bytes 2097152
Async XLA Ops:
  0.0 0.7 %copy-start.5 = (s32[2]{0:T(128)S(1)}, s32[2]{0:T(128)}, u32[]{:S(2)}) copy-start(s32[2]{0:T(128)} %cell_ref.1) | copy-start | bytes 28
  0.0 0.7 %copy-start.3 = (s32[64,2]{0,1:T(2,128)S(1)}, s32[64,2]{0,1:T(2,128)}, u32[]{:S(2)}) copy-start(s32[64,2]{0,1:T(2,128)} %param.7) | copy-start | bytes 1540
  0.7 1.0 %copy-start = (bf16[2,2,16,4096]{3,2,1,0:T(8,128)(2,1)S(1)}, bf16[2,2,16,4096]{3,2,1,0:T(8,128)(2,1)}, u32[]{:S(2)}) copy-start(bf16[2,2,16,4096]{3,2,1,0:T(8,128)(2,1)} %green.1) | copy-start | bytes 1572868
  1.7 0.9 %copy-start.1 = (f32[16,4096]{1,0:T(8,128)S(1)}, f32[16,4096]{1,0:T(8,128)}, u32[]{:S(2)}) copy-start(f32[16,4096]{1,0:T(8,128)} %noise_hbm.1) | copy-start | bytes 786436
  2.7 0.9 %copy-start.2 = (f32[16,4096]{1,0:T(8,128)S(1)}, f32[16,4096]{1,0:T(8,128)}, u32[]{:S(2)}) copy-start(f32[16,4096]{1,0:T(8,128)} %wave_hbm.1) | copy-start | bytes 786436
  3.6 0.7 %copy-start.4 = (f32[2,64]{1,0:T(2,128)S(1)}, f32[2,64]{1,0:T(2,128)}, u32[]{:S(2)}) copy-start(f32[2,64]{1,0:T(2,128)} %values_ref.1) | copy-start | bytes 1540

commit v3 on v2

--- a/solution.py
+++ b/solution.py
@@ -12,7 +12,7 @@
 LANES = 128
 HALO = 8
 ROUNDS = 4
-GROUP = 2
+GROUP = 4
 
 damping = 0.3
 relaxation = 0.8
@@ -92,12 +92,15 @@
     slabs,
     rounds,
     green,
+    pairs_hbm,
+    values_hbm,
+    noise_hbm,
+    wave_hbm,
+    cell_hbm,
+    out,
     pairs_ref,
     values_ref,
-    noise_hbm,
-    wave_hbm,
     cell_ref,
-    out,
     noise,
     wave,
     pieces,
@@ -142,6 +145,13 @@
         pltpu.make_async_copy(noise_hbm, noise, local_sem.at[0]),
         pltpu.make_async_copy(wave_hbm, wave, local_sem.at[1]),
     ]
+    small = [
+        pltpu.make_async_copy(pairs_hbm, pairs_ref, local_sem.at[2]),
+        pltpu.make_async_copy(values_hbm, values_ref, local_sem.at[3]),
+        pltpu.make_async_copy(cell_hbm, cell_ref, local_sem.at[4]),
+    ]
+    for copy in small:
+        copy.start()
     barrier = pltpu.get_barrier_semaphore()
     for mask in order:
         pl.semaphore_signal(
@@ -171,7 +181,7 @@
         other = partner(me, mask)
         return pltpu.make_async_remote_copy(
             src_ref=mixed.at[turn, :, pl.ds(other * owned, owned)],
-            dst_ref=adjoint.at[:, :, :, lanes_of(turn, me)],
+            dst_ref=adjoint.at[turn, me],
             send_sem=send2.at[turn, mask],
             recv_sem=recv2.at[turn, mask],
             device_id={"sta": other},
@@ -236,6 +246,8 @@
     ]
     for copy in own + local_maps:
         copy.start()
+    for copy in small:
+        copy.wait()
     build_mixer(pairs_ref, values_ref, mixer, count, depth)
 
     def wait_maps(mine, theirs, up):
@@ -301,7 +313,7 @@
             )
         for mask in order:
             second_copy(turn, mask).start()
-        adjoint[:, :, :, lanes_of(turn, me)] = mixed[turn, :, pl.ds(me * owned, owned)]
+        adjoint[turn, me] = mixed[turn, :, pl.ds(me * owned, owned)]
 
     columns = lax.broadcasted_iota(jnp.int32, (1, LANES), 1)
     not_first = (columns % GY) != 0
@@ -309,11 +321,15 @@
     upper_half = columns >= GY
     per_part = part // LANES
 
-    def pack(t):
+    def adjoint_at(turn, t, c, k):
+        who = (t - turn * per_part) // (width // LANES)
+        return adjoint[turn, who, c, k, :, tile_of(t % (width // LANES))].astype(f32)
+
+    def pack(turn, t):
         tile = tile_of(t)
         for k in range(owned):
-            re = adjoint[0, k, :, tile].astype(f32)
-            im = adjoint[1, k, :, tile].astype(f32)
+            re = adjoint_at(turn, t, 0, k)
+            im = adjoint_at(turn, t, 1, k)
             edge_out[0, k, :, tile] = jnp.concatenate(
                 [re[depth - HALO :], im[depth - HALO :]], 0
             ).astype(bf16)
@@ -328,7 +344,7 @@
     ids_low = ids_from(-HALO, HALO)
     ids_high = ids_from(depth, HALO)
 
-    def begin(t):
+    def begin(turn, t):
         tile = tile_of(t)
         shifted = tile_of(t + 1)
         step = t * LANES
@@ -337,7 +353,7 @@
             high = edge_in[1, k, :, tile].astype(f32)
 
             def start(power, re, im, ids, s_re, s_im):
-                re = power * re + jnp.where(ids + step == cell_ref[k], point_size, 0.0)
+                re = power * re + jnp.where(ids + step == cell_ref[:, k : k + 1], point_size, 0.0)
                 im = power * im
                 return re, im, s_re * re - s_im * im, s_re * im + s_im * re
 
@@ -353,8 +369,8 @@
 
             main = start(
                 noise[:, tile],
-                adjoint[0, k, :, tile].astype(f32),
-                adjoint[1, k, :, tile].astype(f32),
+                adjoint_at(turn, t, 0, k),
+                adjoint_at(turn, t, 1, k),
                 ids_main,
                 scale_re[:depth, tile],
                 scale_im[:depth, tile],
@@ -376,75 +392,91 @@
                 )
                 source_edge[kc, :, tile] = edge + fix
 
-    def near(old, k, t):
-        v = fields[old][k, :, tile_of(t + 1)]
-        before = fields[old][k, :, tile_of(t)]
-        after = fields[old][k, :, tile_of(t + 2)]
+    def near(before, v, after):
         along_x = pltpu.roll(v + jnp.where(upper_half, before, after), GY, 1)
         left = jnp.where(not_first, pltpu.roll(v, 1, 1), 0.0)
         right = jnp.where(not_last, pltpu.roll(v, LANES - 1, 1), 0.0)
         along_z = pltpu.roll(v, 1, 0) + pltpu.roll(v, tall - 1, 0)
-        return v, along_x + left + right + along_z
+        return along_x + left + right + along_z
 
     kept = 1.0 - relaxation
 
-    def sweep(number, t):
+    def sweep(number, start, tiles):
         old = (number - 1) % 2
         final = number == SWEEPS - 1
         rows = depth if final else tall
-        tile = tile_of(t)
-        s_re = scale_re[:rows, tile]
-        s_im = scale_im[:rows, tile]
+        s_re = [scale_re[:rows, tile_of(start + j)] for j in range(tiles)]
+        s_im = [scale_im[:rows, tile_of(start + j)] for j in range(tiles)]
 
         def pulled(kc):
-            v, n = near(old, kc, t)
-            if number == 1:
-                added = jnp.concatenate([source[kc, :depth, tile], source_edge[kc, :, tile]], 0)
-            else:
-                added = source[kc, :rows, tile]
-            return v[:rows], n[:rows] + added
+            v = [fields[old][kc, :, tile_of(start + j)] for j in range(tiles + 2)]
+            gives = []
+            for j in range(tiles):
+                tile = tile_of(start + j)
+                if number == 1:
+                    added = jnp.concatenate([source[kc, :depth, tile], source_edge[kc, :, tile]], 0)
+                else:
+                    added = source[kc, :rows, tile]
+                n = near(v[j], v[j + 1], v[j + 2])
+                gives.append((kept * v[j + 1][:rows], n[:rows] + added))
+            return gives
 
         for k in range(owned):
-            v_re, n_re = pulled(2 * k)
-            v_im, n_im = pulled(2 * k + 1)
-            re = kept * v_re + (s_re * n_re - s_im * n_im)
-            im = kept * v_im + (s_re * n_im + s_im * n_re)
-            if final:
-                out[0, k, :, tile] = re
-                out[1, k, :, tile] = im
-            else:
-                fields[1 - old][2 * k, :, tile_of(t + 1)] = re
-                fields[1 - old][2 * k + 1, :, tile_of(t + 1)] = im
-
-    def run(low, high, work):
+            real = pulled(2 * k)
+            imag = pulled(2 * k + 1)
+            new = []
+            for j in range(tiles):
+                (v_re, n_re), (v_im, n_im) = real[j], imag[j]
+                new.append(
+                    (
+                        v_re + (s_re[j] * n_re - s_im[j] * n_im),
+                        v_im + (s_re[j] * n_im + s_im[j] * n_re),
+                    )
+                )
+            for j in range(tiles):
+                for c in range(2):
+                    if final:
+                        out[c, k, :, tile_of(start + j)] = new[j][c]
+                    else:
+                        fields[1 - old][2 * k + c, :, tile_of(start + j + 1)] = new[j][c]
+
+    def run_sweep(low, high, number):
         groups = (high - low) // GROUP
 
         def many(g, carry):
-            for j in range(GROUP):
-                work(low + g * GROUP + j)
+            sweep(number, low + g * GROUP, GROUP)
             return carry
 
         if groups:
             lax.fori_loop(0, groups, many, 0)
-        for t in range(low + groups * GROUP, high):
-            work(t)
+        rest = (high - low) % GROUP
+        if rest:
+            sweep(number, high - rest, rest)
+
+    def run(low, high, work, size):
+        def many(g, carry):
+            for j in range(size):
+                work(low + g * size + j)
+            return carry
+
+        lax.fori_loop(0, (high - low) // size, many, 0)
 
     def compute(turn):
         def wait_edge(mine, theirs, up):
             theirs.wait_recv()
 
         each(lambda up: edge_copy(up, turn), wait_edge)
-        run(turn * per_part, (turn + 1) * per_part, begin)
+        run(turn * per_part, (turn + 1) * per_part, functools.partial(begin, turn), 2)
         for number in range(1, SWEEPS):
             low = 0 if turn == 0 else max(turn * per_part - number, 0)
             high = cells // LANES if turn == rounds - 1 else max((turn + 1) * per_part - number, 0)
             if high > low:
-                run(low, high, functools.partial(sweep, number))
+                run_sweep(low, high, number)
 
     for turn in range(rounds):
         for mask in order:
             second_copy(turn, mask).wait_recv()
-        run(turn * per_part, (turn + 1) * per_part, pack)
+        run(turn * per_part, (turn + 1) * per_part, functools.partial(pack, turn), 4)
 
         def start_edge(mine, theirs, up):
             mine.start()
@@ -473,19 +505,22 @@
     tall = depth + HALO
     size = 2 * count * depth
     vmem = pl.BlockSpec(memory_space=pltpu.VMEM)
-    hbm = pl.BlockSpec(memory_space=pl.ANY)
+    hbm = pl.BlockSpec(memory_space=pltpu.HBM)
     dma = pltpu.SemaphoreType.DMA
     return pl.pallas_call(
         functools.partial(kernel, n, slabs, rounds),
         out_shape=jax.ShapeDtypeStruct((2, owned, depth, cells), f32),
-        in_specs=[hbm, vmem, vmem, hbm, hbm, pl.BlockSpec(memory_space=pltpu.SMEM)],
+        in_specs=[hbm] * 6,
         out_specs=vmem,
         scratch_shapes=[
+            pltpu.VMEM(pair_list.shape[::-1], jnp.int32),
+            pltpu.VMEM(pair_values.shape, f32),
+            pltpu.VMEM((1, owned), jnp.int32),
             pltpu.VMEM((depth, cells), f32),
             pltpu.VMEM((depth, cells), f32),
             pltpu.VMEM((rounds, 2, count, depth, width), bf16),
             pltpu.VMEM((rounds, 2, count, depth, width), bf16),
-            pltpu.VMEM((2, owned, depth, cells), bf16),
+            pltpu.VMEM((rounds, n, 2, owned, depth, width), bf16),
             pltpu.VMEM((size, size), bf16),
             pltpu.VMEM((2, owned, 2 * HALO, cells), bf16),
             pltpu.VMEM((2, owned, 2 * HALO, cells), bf16),
@@ -506,12 +541,12 @@
             dma((2, 2)),
             dma((2, 2)),
             dma((rounds,)),
-            dma((2,)),
+            dma((5,)),
         ],
         compiler_params=pltpu.CompilerParams(
-            collective_id=0, has_side_effects=True, vmem_limit_bytes=48 * 1024 * 1024
+            collective_id=0, has_side_effects=True, vmem_limit_bytes=62 * 1024 * 1024
         ),
-    )(green_fields, pair_list.T, pair_values, noise_map, wave_square, station_cell)
+    )(green_fields, pair_list.T, pair_values, noise_map, wave_square, station_cell[None, :])
 
 
 def solution(mesh):

time: 48.4 us -> 43.7 us (0.903)
  local copies, waits for them, and re-layouts: 5.28 us -> 2.27 us
  Pallas kernels: 42.9 us -> 41.2 us
    unnamed x13 -> x1, local copies, waits for them, and re-layouts: 5.28 us -> 2.27 us
    pallas_call x1, Pallas kernels: 42.9 us -> 41.2 us  [local(): pl.pallas_call(functools.partial(kernel, n, slabs, rounds), out_shape=jax...]
where the time goes in v3:
time: 43.7 us; the launch traced here: 43.5 us
  Pallas kernels  41.2 us (94%)
  local copies, waits for them, and re-layouts  2.27 us (5%)
    pallas_call x1, Pallas kernels, local(): pl.pallas_call(functools.partial(kernel, n, slabs, rounds), out_shape=jax...  41.2 us
    unnamed x1, local copies, waits for them, and re-layouts  2.27 us

profile of v3, /device:TPU:1, one launch (start us, length us, event | category | flops | bytes accessed | tf_op | source)
XLA Modules:
  0.0 43.5 jit_solution(2764178118385609332)
XLA Ops:
  0.0 41.2 %shard_map.64 = f32[2,2,16,4096]{3,2,1,0:T(8,128)} custom-call(bf16[2,2,16,4096]{3,2,1,0:T(8,128)(2,1)} %green.1, s32[2,64]{1,0:T(2,128)} %bitcast.2, f32[2,64]{1,0:T(2,128)} %values_hbm.1, f32[16,4096]{1,0:T(8,128)} %noise_hbm.1, f32[16,4096]{1,0:T(8,128)} %wave_hbm.1, s32[1,2]{1,0:T(1,128)} %bitcast.3), custom_call_target="tpu_custom_call" | custom-call | tf_op jit(solution)/shard_map/pallas_call | solution.py:510
  41.3 2.3 %copy.8 = f32[2,2,16,4096]{3,2,1,0:T(8,128)} copy(f32[2,2,16,4096]{3,2,1,0:T(8,128)} %shard_map.64) | data formatting | bytes 2097152

commit v4 on v3

--- a/solution.py
+++ b/solution.py
@@ -11,7 +11,7 @@
 SWEEPS = 6
 LANES = 128
 HALO = 8
-ROUNDS = 4
+ROUNDS = 2
 GROUP = 4
 
 damping = 0.3

time: 43.7 us -> 45.2 us (1.034); the launches traced: 43.5 us -> 44.5 us
  Pallas kernels: 41.2 us -> 42.3 us
    pallas_call x1, Pallas kernels: 41.2 us -> 42.3 us  [local(): pl.pallas_call(functools.partial(kernel, n, slabs, rounds), out_shape=jax...]
where the time goes in v4:
time: 45.2 us; the launch traced here: 44.5 us
  Pallas kernels  42.3 us (94%)
  local copies, waits for them, and re-layouts  2.27 us (5%)
    pallas_call x1, Pallas kernels, local(): pl.pallas_call(functools.partial(kernel, n, slabs, rounds), out_shape=jax...  42.3 us
    unnamed x1, local copies, waits for them, and re-layouts  2.27 us

profile of v4, /device:TPU:1, one launch (start us, length us, event | category | flops | bytes accessed | tf_op | source)
XLA Modules:
  0.0 44.5 jit_solution(11899291330116667748)
XLA Ops:
  0.0 42.3 %shard_map.64 = f32[2,2,16,4096]{3,2,1,0:T(8,128)} custom-call(bf16[2,2,16,4096]{3,2,1,0:T(8,128)(2,1)} %green.1, s32[2,64]{1,0:T(2,128)} %bitcast.2, f32[2,64]{1,0:T(2,128)} %values_hbm.1, f32[16,4096]{1,0:T(8,128)} %noise_hbm.1, f32[16,4096]{1,0:T(8,128)} %wave_hbm.1, s32[1,2]{1,0:T(1,128)} %bitcast.3), custom_call_target="tpu_custom_call" | custom-call | tf_op jit(solution)/shard_map/pallas_call | solution.py:510
  42.3 2.3 %copy.8 = f32[2,2,16,4096]{3,2,1,0:T(8,128)} copy(f32[2,2,16,4096]{3,2,1,0:T(8,128)} %shard_map.64) | data formatting | bytes 2097152
